TPU v7x, 512 devices: a whole 4x8x8 slice. The times are simulated.
512 devices in a mesh: dp: 64 (over x, y, core), tensor: 8 (over z).
Axes of the slice: x: 4, y: 8, z: 8, core: 2. Of those that a mesh axis runs over, the one named last changes fastest.
Arguments:
- tokens: bfloat16 [8192, 8192], P('dp', 'tensor'), may hold values from -6 to 6
- value_weight: bfloat16 [8192, 1024], P('tensor'), may hold values from -0.0625 to 0.0625
- down_panels: bfloat16 [64, 8192, 64], P('dp', 'tensor'), may hold values from -0.0625 to 0.0625
- up_panels: bfloat16 [64, 64, 1024], P('dp', None, 'tensor'), may hold values from -0.1875 to 0.1875
- output_gradient: bfloat16 [8192, 1024], P('dp', 'tensor'), may hold values from -6 to 6
- sequence_adapter: int32 [512, 1], P('dp'), may hold values from 0 to 63
- sequence_lengths: int32 [64, 8], P('dp'), may hold values from 1 to 64, 128 in all within a row
- owner_slot_table: int32 [64], replicated, may hold values from 0 to 63, each once
Outputs:
- values: bfloat16 [8192, 1024], P('dp', 'tensor')
- token_gradient: bfloat16 [8192, 8192], P('dp', 'tensor')
- grad_a: float32 [64, 8192, 64], P('dp', 'tensor')
- grad_b: float32 [64, 64, 1024], P('dp', None, 'tensor')
Inputs may be any that keep to these rules, and one draw needn't show every extreme that they name: `sequence_adapter`: every adapter id is named by at least one sequence. `sequence_lengths`: each row sums to 128; some entry equals 64. `owner_slot_table`: each slot appears exactly once.
All inputs are finite; a program needn't handle non-finite values.
Results may differ from a plain program's by a relative error of at most 0.0075.
Values may be sent and summed in bfloat16 or wider, within the bound.
A program may use at most 64 MiB of HBM per device.

v0:
```python
import jax
import jax.numpy as jnp
from jax import lax
from jax.sharding import PartitionSpec as P

ADAPTER_SCALE = 2.0


def shards(
    tokens,
    value_weight,
    down_panels,
    up_panels,
    output_gradient,
    sequence_adapter,
    sequence_lengths,
    owner_slot_table,
):
    groups = lax.axis_size("dp")
    tok_rows, local_width = tokens.shape
    kept_panels, unused_result, rank_extent = down_panels.shape
    local_value_output = up_panels.shape[2]
    seq_count = sequence_adapter.shape[0]
    adapter_total = owner_slot_table.shape[0]
    down_panel_count = local_width * rank_extent
    panel_len = down_panel_count + rank_extent * local_value_output
    piece_len = panel_len // groups
    base_terms = jnp.dot(tokens, value_weight, preferred_element_type=jnp.float32)
    base_values = lax.psum_scatter(base_terms, "tensor", scatter_dimension=1, tiled=True)
    frozen_gradient = lax.dot_general(
        lax.all_gather(output_gradient, "tensor", axis=1, tiled=True),
        value_weight,
        (((1,), (1,)), ((), ())),
        preferred_element_type=jnp.float32,
    )
    adapter_hits = (
        sequence_adapter[:, 0][:, None] == jnp.arange(adapter_total, dtype=jnp.int32)[None, :]
    )
    my_slots = jnp.sum(jnp.where(adapter_hits, owner_slot_table[None, :], 0), axis=1)
    every_slot = lax.all_gather(my_slots, "dp", axis=0, tiled=True)
    own_panels = jnp.concatenate(
        [
            down_panels.reshape(kept_panels, down_panel_count),
            up_panels.reshape(kept_panels, rank_extent * local_value_output),
        ],
        axis=1,
    )
    piece = lax.all_gather(own_panels, "dp", axis=0, tiled=True)
    slot_ids = jnp.arange(piece.shape[0], dtype=jnp.int32)
    select = (my_slots[:, None] == slot_ids[None, :]).astype(jnp.bfloat16)
    fetched = jnp.dot(select, piece, preferred_element_type=jnp.float32).astype(jnp.bfloat16)
    down_joined = jnp.transpose(
        fetched[:, :down_panel_count].reshape(seq_count, local_width, rank_extent), (1, 0, 2)
    )
    down_joined = down_joined.reshape(local_width, seq_count * rank_extent)
    up_joined = fetched[:, down_panel_count:].reshape(seq_count * rank_extent, local_value_output)
    seg_ends = jnp.cumsum(sequence_lengths[0])
    position = jnp.arange(tok_rows, dtype=jnp.int32)
    segment = jnp.sum((position[:, None] >= seg_ends[None, :]).astype(jnp.int32), axis=1)
    sequence_mask = (segment[:, None] == jnp.arange(seq_count, dtype=jnp.int32)[None, :]).astype(
        jnp.float32
    )

    def grouped(wide):
        return jnp.sum(
            wide.reshape(tok_rows, seq_count, rank_extent) * sequence_mask[:, :, None], axis=1
        )

    def expanded_rows(narrow):
        wide = narrow[:, None, :] * sequence_mask[:, :, None].astype(jnp.bfloat16)
        return wide.reshape(tok_rows, seq_count * rank_extent)

    down_part = grouped(jnp.dot(tokens, down_joined, preferred_element_type=jnp.float32))
    back_part = grouped(
        lax.dot_general(
            output_gradient, up_joined, (((1,), (1,)), ((), ())), preferred_element_type=jnp.float32
        )
    )
    down_total, backward_total = lax.psum((down_part, back_part), "tensor")
    rank_activations = expanded_rows((ADAPTER_SCALE * down_total).astype(jnp.bfloat16))
    rank_gradient = expanded_rows((ADAPTER_SCALE * backward_total).astype(jnp.bfloat16))
    values = (
        base_values + jnp.dot(rank_activations, up_joined, preferred_element_type=jnp.float32)
    ).astype(jnp.bfloat16)
    adapter_backward = lax.dot_general(
        rank_gradient, down_joined, (((1,), (1,)), ((), ())), preferred_element_type=jnp.float32
    )
    token_gradient = (frozen_gradient + adapter_backward).astype(jnp.bfloat16)
    rows_term = lax.dot_general(
        tokens, rank_gradient, (((0,), (0,)), ((), ())), preferred_element_type=jnp.float32
    )
    rows_term = jnp.transpose(
        rows_term.reshape(local_width, seq_count, rank_extent), (1, 0, 2)
    ).reshape(seq_count, down_panel_count)
    cols_term = lax.dot_general(
        rank_activations,
        output_gradient,
        (((0,), (0,)), ((), ())),
        preferred_element_type=jnp.float32,
    )
    seg_grads = jnp.concatenate(
        [rows_term, cols_term.reshape(seq_count, rank_extent * local_value_output)], axis=1
    )
    arrived = lax.all_to_all(
        seg_grads.reshape(seq_count, groups, piece_len),
        "dp",
        split_axis=1,
        concat_axis=0,
        tiled=True,
    )
    arrived = arrived.reshape(groups * seq_count, piece_len)
    owner_hits = (
        jnp.arange(adapter_total, dtype=jnp.int32)[:, None] == every_slot[None, :]
    ).astype(jnp.float32)
    summed = jnp.dot(
        owner_hits, arrived, precision=lax.Precision.HIGHEST, preferred_element_type=jnp.float32
    )
    returned = lax.all_to_all(
        summed.reshape(groups, kept_panels, piece_len),
        "dp",
        split_axis=0,
        concat_axis=2,
        tiled=True,
    )
    returned = returned.reshape(kept_panels, panel_len)
    grad_a = returned[:, :down_panel_count].reshape(kept_panels, local_width, rank_extent)
    grad_b = returned[:, down_panel_count:].reshape(kept_panels, rank_extent, local_value_output)
    return (values, token_gradient, grad_a, grad_b)


def solution(mesh):
    placed = (
        P("dp", "tensor"),
        P("tensor", None),
        P("dp", "tensor", None),
        P("dp", None, "tensor"),
        P("dp", "tensor"),
        P("dp", None),
        P("dp", None),
        P(),
    )
    return jax.shard_map(
        shards,
        mesh=mesh,
        in_specs=placed,
        out_specs=(
            P("dp", "tensor"),
            P("dp", "tensor"),
            P("dp", "tensor", None),
            P("dp", None, "tensor"),
        ),
        check_vma=False,
    )
```

profile of v0, /device:TPU:1, one launch (start us, length us, event | category | flops | bytes accessed | tf_op | source)
XLA Modules:
  0.0 382.0 jit_solution(10764491726688869215)
XLA Ops:
  7.2 1.2 copy.22
  12.9 114.5 %all-gather.3.cloned.1.call-done = bf16[64,1,73728]{2,1,0:T(2,128)(2,1)} async-done(((bf16[1,1,73728]{2,1,0:T(2,128)(2,1)}), bf16[64,1,73728]{2,1,0:T(2,128)(2,1)}) %all-gather.3.cloned.1.call-update) | async-done | bytes 9437200 | tf_op jit(solution)/shard_map/all_gather | solution.py:48
  127.4 16.3 %convolution_convert_fusion = bf16[8,73728]{1,0:T(8,128)(2,1)S(1)} fusion(bf16[64,1,73728]{2,1,0:T(2,128)(2,1)} %all-gather.3.cloned.1.call-done, s32[8]{0:T(128)S(1)} %select_reduce_fusion), kind=kOutput, calls=%fused_computation | convolution fusion | flops 76087808 | bytes 10616864 | tf_op jit(solution)/shard_map/dot_general | solution.py:51
  144.7 3.7 reshape.151
  148.4 1.9 copy.23
  151.5 1.1 fusion.16
  153.3 70.3 %all-reduce.4.cloned.1.call-done = (f32[128,64]{0,1:T(8,128)}, f32[128,64]{0,1:T(8,128)}) async-done(((f32[128,64]{0,1:T(8,128)}, f32[128,64]{0,1:T(8,128)}), (f32[128,64]{0,1:T(8,128)}, f32[128,64]{0,1:T(8,128)})) %all-reduce.4.cloned.1.call-update) | async-done | bytes 65552 | tf_op jit(solution)/shard_map/psum | solution.py:79
  226.5 1.6 fusion.18
  228.1 1.7 reshape.160
  229.8 1.7 fusion.17
  231.6 3.8 copy.24
  235.3 4.7 %reshape.159 = f32[8,65536]{1,0:T(8,128)} reshape(f32[8,1024,64]{2,1,0:T(8,128)} %bitcast.60) | data formatting | bytes 4194304 | tf_op jit(solution)/shard_map/reshape | solution.py:94
  240.1 3.3 pad_maximum_fusion
  243.3 15.1 %all-to-all-start = ((f32[8,64,1152]{2,0,1:T(8,128)}), f32[8,64,1152]{2,0,1:T(8,128)}, u32[]{:S(2)}, u32[]{:S(2)}) async-start(f32[8,64,1152]{2,0,1:T(8,128)} %bitcast.62), calls=%async_computation.1 | async-start | bytes 4718592 | tf_op jit(solution)/shard_map/all_to_all | solution.py:104
  258.5 1.3 fusion.14
  259.8 1.3 dynamic-slice
  262.0 61.1 %all-reduce = s32[512]{0:T(512)S(1)} all-reduce(s32[512]{0:T(512)S(1)} %dynamic-update-slice), channel_id=1, replica_groups=mesh['dp'=64,'tensor'=8] {'dp'}, use_global_device_ids=true, to_apply=%add | all-reduce | flops 512 | bytes 4096
  323.1 18.6 %all_gather.10 = bf16[128,1024]{1,0:T(8,128)(2,1)} all-gather(bf16[128,128]{1,0:T(8,128)(2,1)S(1)} %copy-done.4), channel_id=1, replica_groups=mesh['dp'=64,'tensor'=8] {'tensor'}, dimensions={1}, use_global_device_ids=true | all-gather | bytes 294912 | tf_op jit(solution)/shard_map/all_gather | solution.py:31
  341.7 2.7 fusion.4
  345.4 15.1 %all-to-all-start.1 = ((f32[64,1,1152]{2,1,0:T(1,128)}), f32[64,1,1152]{2,1,0:T(1,128)S(1)}, u32[]{:S(2)}, u32[]{:S(2)}) async-start(f32[64,1,1152]{2,1,0:T(1,128)} %copy.25), calls=%async_computation.2 | async-start | bytes 589824 | tf_op jit(solution)/shard_map/all_to_all | solution.py:118
  360.5 1.1 convolution_bitcast_fusion
  361.6 1.8 fusion.8
  363.5 2.7 fusion.7
  366.1 7.1 %all-to-all-done.1 = f32[64,1,1152]{2,1,0:T(1,128)S(1)} async-done(((f32[64,1,1152]{2,1,0:T(1,128)}), f32[64,1,1152]{2,1,0:T(1,128)S(1)}, u32[]{:S(2)}, u32[]{:S(2)}) %all-to-all-start.1) | async-done | bytes 294944 | tf_op jit(solution)/shard_map/all_to_all | solution.py:118
  (47 shorter events, 13.8 us)
Async XLA Ops:
  7.2 251.3 %copy-start = (bf16[1024,1024]{1,0:T(8,128)(2,1)S(1)}, bf16[1024,1024]{1,0:T(8,128)(2,1)}, u32[]{:S(2)}) copy-start(bf16[1024,1024]{1,0:T(8,128)(2,1)} %param.9) | copy-start | bytes 6291460
  7.2 120.2 %all-gather.3.cloned.1.call-start = ((), (), s32[]{:S(2)}) async-start(), calls=%async_computation.4 | async-start | bytes 19169280 | tf_op jit(solution)/shard_map/all_gather | solution.py:48
  10.4 213.2 %all-reduce.4.cloned.1.call-start = ((), (), s32[]{:S(2)}) async-start(), calls=%async_computation.5 | async-start | bytes 131072 | tf_op jit(solution)/shard_map/psum | solution.py:79
  12.3 131.4 %copy-start.6 = (s32[8]{0:T(128)}, s32[8]{0:T(128)S(1)}, u32[]{:S(2)}) copy-start(s32[8]{0:T(128)S(1)} %select_reduce_fusion) | copy-start | bytes 100
  143.7 1.0 copy-start.1
  148.4 2.0 slice-start
  148.4 2.7 copy-start.2
  225.8 0.7 copy-start.3
  243.3 98.4 %all-to-all-start = ((f32[8,64,1152]{2,0,1:T(8,128)}), f32[8,64,1152]{2,0,1:T(8,128)}, u32[]{:S(2)}, u32[]{:S(2)}) async-start(f32[8,64,1152]{2,0,1:T(8,128)} %bitcast.62), calls=%async_computation.1 | async-start | bytes 4718592 | tf_op jit(solution)/shard_map/all_to_all | solution.py:104
  258.4 3.3 copy-start.7
  258.4 64.7 %copy-start.4 = (bf16[128,128]{1,0:T(8,128)(2,1)S(1)}, bf16[128,128]{1,0:T(8,128)(2,1)}, u32[]{:S(2)}) copy-start(bf16[128,128]{1,0:T(8,128)(2,1)} %param.12) | copy-start | bytes 98308
  258.5 103.2 %reduce-scatter.2.cloned.1.call-start = ((), (), s32[]{:S(2)}) async-start(), calls=%async_computation.3 | async-start | bytes 589824 | tf_op jit(solution)/shard_map/reduce_scatter | solution.py:29
  259.8 100.7 %copy-start.5 = (bf16[128,8]{0,1:T(8,128)(2,1)S(1)}, bf16[128,8]{0,1:T(8,128)(2,1)}, u32[]{:S(2)}) copy-start(bf16[128,8]{0,1:T(8,128)(2,1)} %get-tuple-element.23) | copy-start | bytes 6148
  345.4 27.7 %all-to-all-start.1 = ((f32[64,1,1152]{2,1,0:T(1,128)}), f32[64,1,1152]{2,1,0:T(1,128)S(1)}, u32[]{:S(2)}, u32[]{:S(2)}) async-start(f32[64,1,1152]{2,1,0:T(1,128)} %copy.25), calls=%async_computation.2 | async-start | bytes 589824 | tf_op jit(solution)/shard_map/all_to_all | solution.py:118
Sparse Core Ops, SparseCore 0:
  11.3 115.9 all-gather.2
  153.4 70.1 all-reduce.3
  262.3 35.0 reduce-scatter.1
where the time goes:
time: 383 us; the launch traced here: 382 us
  waiting for transfers between devices  192 us (50%)
  blocking collectives  79.7 us (21%)
  matrix products  30.7 us (8%)
  starting transfers between devices  30.3 us (8%)
  local copies, waits for them, and re-layouts  25.2 us (7%)
  between operations  14.6 us (4%)
  other arithmetic  9.58 us (3%)
    all_gather x1, waiting for transfers between devices, shards(): piece = lax.all_gather(own_panels, 'dp', axis=0, tiled=True)  115 us
    psum x1, waiting for transfers between devices, shards(): down_total, backward_total = lax.psum((down_part, back_part), 'tensor')  70.3 us
    unnamed x1, blocking collectives  61.1 us
    all_gather x1, blocking collectives, shards(): lax.all_gather(output_gradient, 'tensor', axis=1, tiled=True)  18.6 us
    dot_general x1, matrix products, shards(): jnp.dot(select, piece, preferred_element_type=jnp.float32)  16.3 us
    all_to_all x1, starting transfers between devices, shards(): lax.all_to_all(seg_grads.reshape(seq_count, groups, piece_len), 'dp', spl...  15.1 us
    all_to_all x1, starting transfers between devices, shards(): lax.all_to_all(summed.reshape(groups, kept_panels, piece_len), 'dp', spli...  15.1 us
  transfers between devices with their start and end apart: 5, of which 3 were waited for; matrix products, arithmetic and copies ran while one was open for 4% of the time, Pallas kernels for 0%

commit v1 on v0

v1 whole, which is shorter than its diff:
```python
import functools

import jax
import jax.numpy as jnp
from jax import lax
from jax.experimental import pallas as pl
from jax.experimental.pallas import tpu as pltpu
from jax.sharding import PartitionSpec as P

MESH = pl.DeviceIdType.MESH
BF = jnp.bfloat16
F32 = jnp.float32
NT = (((1,), (1,)), ((), ()))
T = 128
R = 64
C = 128

(S_DT, S_DY, S_SL, S_X, S_DYZ, S_U, S_LGP, S_LGZ, S_LGR, S_BZ, S_LRP, S_LRZ, S_LRR, S_TG, S_VC, S_GB, S_GA) = range(17)
N_STAGES = 17


def ring_steps(ny, d, h):
    return ny // 2 if d == h else ny - 1 - ny // 2


def kernel(
    nx, ny, nz,
    x_hbm, w_hbm, dt_hbm, u_hbm, dy_hbm, adp, lens, tab,
    v_out, tg_out, ga_out, gb_out,
    xv, wv, xr, dg, dyr, slw, slo, dyf, ug,
    lgps, lgp, lgzs, lgz, lgs, lgt,
    bs, bz, fz,
    lracc, lrps, lrp, lrzs, lrz, lrs, lrt,
    mbig, mt, two, st, tgacc, tgs, tgc, vcs, vc, pbs, gbp,
    pa, pas, rb, fin,
    ss, rs, ag_s, ag_r, rs_s, rs_r, ld,
):
    rw = 2 * nx
    hw = rw // 2
    me = lax.axis_index("dp")
    z = lax.axis_index("tensor")
    c = me % 2
    y = (me // 2) % ny
    x = me // (2 * ny)
    j = x * 2 + c

    def row_dev(jj):
        return (jj // 2) * (2 * ny) + y * 2 + jj % 2

    def y_dev(yy):
        return x * (2 * ny) + yy * 2 + c

    def slot_id(jj, yy):
        return (jj // 2) * (2 * ny) + yy * 2 + jj % 2

    def col(i):
        return pl.ds(pl.multiple_of(i * 128, 128), 128)

    def rcopy(src, dst, s, r, dev):
        return pltpu.make_async_remote_copy(
            src_ref=src, dst_ref=dst, send_sem=s, recv_sem=r, device_id=dev, device_id_type=MESH
        )

    def exchange(n, mine, dev, src, dst, stage):
        @pl.loop(1, n)
        def _(i):
            q = (mine + i) % n
            rcopy(src(q), dst, ss.at[stage], rs.at[stage], dev(q)).start()

        pltpu.make_async_copy(src(mine), dst, rs.at[stage]).start()

    def row_exchange(src, dst, stage):
        exchange(rw, j, lambda q: (row_dev(q), z), src, dst, stage)

    def y_exchange(src, dst, stage):
        exchange(ny, y, lambda q: (y_dev(q), z), src, dst, stage)

    def z_exchange(src, dst, stage):
        exchange(nz, z, lambda q: (me, q), src, dst, stage)

    def got(ref, stage):
        pltpu.make_async_copy(ref, ref, rs.at[stage]).wait()

    barrier = pltpu.get_barrier_semaphore()

    @pl.loop(1, rw)
    def _(i):
        pl.semaphore_signal(barrier, inc=1, device_id=(row_dev((j + i) % rw), z), device_id_type=MESH)

    @pl.loop(1, ny)
    def _(i):
        pl.semaphore_signal(barrier, inc=1, device_id=(y_dev((y + i) % ny), z), device_id_type=MESH)

    @pl.loop(1, nz)
    def _(i):
        pl.semaphore_signal(barrier, inc=1, device_id=(me, (z + i) % nz), device_id_type=MESH)

    load_w = pltpu.make_async_copy(w_hbm, wv, ld.at[0])
    load_x = pltpu.make_async_copy(x_hbm, xv, ld.at[1])
    load_x.start()
    load_w.start()

    position = lax.broadcasted_iota(jnp.int32, (8, T), 1)
    slots = jnp.full((8, T), 0, jnp.int32)
    begin = jnp.int32(0)
    for k in range(8):
        slots = jnp.where(position >= begin, tab[adp[k]], slots)
        begin = begin + lens[k]
    slo[...] = slots

    pl.semaphore_wait(barrier, rw + ny + nz - 3)

    y_exchange(lambda q: u_hbm, ug.at[y], S_U)
    row_exchange(lambda q: dt_hbm.at[:, col(q)], dg.at[y, j], S_DT)
    row_exchange(lambda q: slo, slw.at[:, col(j)], S_SL)
    row_exchange(lambda q: dy_hbm, dyr.at[j], S_DY)
    row_exchange(lambda q: x_hbm.at[:, col(q)], xr.at[j], S_X)
    z_exchange(lambda q: dy_hbm, dyf.at[:, col(z)], S_DYZ)

    load_x.wait()
    load_w.wait()

    @pl.loop(0, nz // 2)
    def _(i):
        part = jnp.dot(
            xv[...], wv[:, pl.ds(pl.multiple_of(i * 256, 256), 256)], preferred_element_type=F32
        ).astype(BF)
        bs[2 * i] = part[:, :C]
        bs[2 * i + 1] = part[:, C:]

    z_exchange(lambda q: bs.at[q], bz.at[z], S_BZ)

    def half(h):
        return pl.ds(h * hw, hw)

    def ag_copy(d, h, s):
        yy = (y - (s - 1) if d == 0 else y + (s - 1)) % ny
        to = (y + 1 if d == 0 else y - 1) % ny
        block = dg.at[yy, half(h)]
        return rcopy(block, block, ag_s.at[d, h, s - 1], ag_r.at[d, h, s - 1], (y_dev(to), z))

    def ag_send(s):
        for h in range(2):
            for d in range(2):
                if s <= ring_steps(ny, d, h):
                    ag_copy(d, h, s).start()

    def ag_got(s):
        for h in range(2):
            for d in range(2):
                if s <= ring_steps(ny, d, h):
                    yy = (y - s if d == 0 else y + s) % ny
                    block = dg.at[yy, half(h)]
                    pltpu.make_async_copy(block, block, ag_r.at[d, h, s - 1]).wait()
                    if s + 1 <= ring_steps(ny, d, h):
                        ag_copy(d, h, s + 1).start()

    got(dg.at[y], S_DT)
    ag_send(1)

    got(ug, S_U)
    got(slw, S_SL)
    got(dyr, S_DY)

    @pl.loop(0, rw)
    def _(b):
        wide = lax.dot_general(
            ug[...].reshape(ny * R, C), dyr[b], NT, preferred_element_type=F32
        )
        of = slw[0:1, col(b)]
        total = jnp.zeros((R, T), F32)
        for yy in range(ny):
            total = total + jnp.where(of == slot_id(j, yy), wide[yy * R : (yy + 1) * R], 0.0)
        lgps[b] = total.astype(BF)

    row_exchange(lambda q: lgps.at[q], lgp.at[j], S_LGP)

    got(dyf, S_DYZ)

    @pl.loop(0, rw // 2)
    def _(i):
        f = pl.ds(pl.multiple_of(i * 256, 256), 256)
        fz[:, f] = lax.dot_general(dyf[...], wv[f, :], NT, preferred_element_type=F32)

    def sum_of(ref, n):
        total = ref[0].astype(F32)
        for i in range(1, n):
            total = total + ref[i].astype(F32)
        return total

    got(lgp, S_LGP)
    lgzs[...] = sum_of(lgp, rw).astype(BF)
    z_exchange(lambda q: lgzs, lgz.at[z], S_LGZ)

    ag_got(1)

    got(lgz, S_LGZ)
    lgs[...] = (2.0 * sum_of(lgz, nz)).astype(BF)
    row_exchange(lambda q: lgs, lgt.at[:, col(j)], S_LGR)

    got(xr, S_X)

    @pl.loop(0, rw)
    def _(b):
        of = jnp.broadcast_to(slw[0:1, col(b)].astype(F32), (T, T))
        st[pl.ds(pl.multiple_of(b * T, T), T), :] = of.T
        lracc[b] = jnp.zeros((R, T), F32)

    def low_rank_chunk(yy):
        panels = dg[yy].reshape(rw * R, C)

        @pl.loop(0, rw // 2)
        def _(i):
            pair = xr[pl.ds(2 * i, 2)].reshape(2 * T, C)
            wide = lax.dot_general(panels, pair, NT, preferred_element_type=F32)
            for e in range(2):
                of = slw[0:1, col(2 * i + e)]
                total = lracc[2 * i + e]
                for k in range(rw):
                    total = total + jnp.where(
                        of == slot_id(k, yy), wide[k * R : (k + 1) * R, e * T : (e + 1) * T], 0.0
                    )
                lracc[2 * i + e] = total

    if ny > 2:
        ag_got(2)
    low_rank_chunk(y)

    got(lgt, S_LGR)

    def grad_chunk(yy):
        of = slw[0:1, :]
        lg = lgt[...].astype(F32)
        for k in range(rw):
            mbig[k * R : (k + 1) * R, :] = jnp.where(of == slot_id(k, yy), lg, 0.0).astype(BF)
        pa[yy] = jnp.dot(mbig[: rw * R, :], xr[...].reshape(rw * T, C), preferred_element_type=F32)

    def hrows(h):
        return pl.ds(h * hw * R, hw * R)

    def rs_copy(d, h, s):
        n = ring_steps(ny, d, h)
        dest = (y + (n - s + 1) if d == 0 else y - (n - s + 1)) % ny
        to = (y + 1 if d == 0 else y - 1) % ny
        return rcopy(
            pas.at[dest, hrows(h)], rb.at[d, h, s - 1], rs_s.at[d, h, s - 1], rs_r.at[d, h, s - 1], (y_dev(to), z)
        )

    def rs_send(d, h, s):
        n = ring_steps(ny, d, h)
        if s > n:
            return
        dest = (y + (n - s + 1) if d == 0 else y - (n - s + 1)) % ny
        part = pa[dest, hrows(h)]
        if s > 1:
            rs_got(d, h, s - 1)
            part = part + rb[d, h, s - 2].astype(F32)
        pas[dest, hrows(h)] = part.astype(BF)
        rs_copy(d, h, s).start()

    def rs_got(d, h, s):
        block = rb.at[d, h, s - 1]
        pltpu.make_async_copy(block, block, rs_r.at[d, h, s - 1]).wait()

    far = ny // 2
    grad_chunk((y + far) % ny)
    for d in range(2):
        rs_send(d, d, 1)
    if far > 1:
        grad_chunk((y + far - 1) % ny)
        grad_chunk((y - far + 1) % ny)
        for d in range(2):
            rs_send(d, 1 - d, 1)
    low_rank_chunk((y + 1) % ny)
    if ny > 2:
        low_rank_chunk((y - 1) % ny)
    for s in range(3, far + 1):
        ag_got(s)
    for s in range(2, far + 1):
        for d in range(2):
            rs_send(d, d, s)
        if far - s > 0:
            grad_chunk((y + far - s) % ny)
            grad_chunk((y - far + s) % ny)
            for d in range(2):
                rs_send(d, 1 - d, s)
    grad_chunk(y)
    for s in range(2, far):
        low_rank_chunk((y + s) % ny)
        low_rank_chunk((y - s) % ny)
    if far > 1:
        low_rank_chunk((y + far) % ny)

    @pl.loop(0, rw)
    def _(b):
        lrps[b] = lracc[b].astype(BF)

    row_exchange(lambda q: lrps.at[q], lrp.at[j], S_LRP)

    for h in range(2):
        total = pa[y, hrows(h)]
        for d in range(2):
            n = ring_steps(ny, d, h)
            if n > 0:
                rs_got(d, h, n)
                total = total + rb[d, h, n - 1].astype(F32)
        for k in range(hw):
            fin[h * hw + k] = total[k * R : (k + 1) * R]
    row_exchange(lambda q: fin.at[q], ga_out.at[:, col(j)], S_GA)

    got(lrp, S_LRP)
    lrzs[...] = sum_of(lrp, rw).astype(BF)
    z_exchange(lambda q: lrzs, lrz.at[z], S_LRZ)

    lane = lax.broadcasted_iota(jnp.int32, (T, 128), 1)

    def rows_of(b):
        return pl.ds(pl.multiple_of(b * T, T), T)

    def doubled(src):
        @pl.loop(0, rw)
        def _(b):
            one = src[:, col(b)].astype(F32)
            two[rows_of(b), :] = jnp.concatenate([one, one], axis=0).T

    def spread(ids):
        @pl.loop(0, rw)
        def _(b):
            of = st[rows_of(b), :]
            rows = two[rows_of(b), :]
            for m in range(len(ids) // 2):
                want = jnp.where(lane < R, ids[2 * m], ids[2 * m + 1]).astype(F32)
                mt[rows_of(b), m * 128 : (m + 1) * 128] = jnp.where(of == want, rows, 0.0).astype(BF)

    doubled(lgt)
    tgacc[...] = jnp.zeros_like(tgacc)

    @pl.loop(0, ny)
    def _(yy):
        spread([slot_id(k, yy) for k in range(rw)])
        tgacc[...] += jnp.dot(
            mt[:, : rw * R], dg[yy].reshape(rw * R, C), preferred_element_type=F32
        )

    tgs[...] = tgacc[...].astype(BF).reshape(rw, T, C)
    row_exchange(lambda q: tgs.at[q], tgc.at[j], S_TG)

    got(lrz, S_LRZ)
    lrs[...] = (2.0 * sum_of(lrz, nz)).astype(BF)
    row_exchange(lambda q: lrs, lrt.at[:, col(j)], S_LRR)

    got(tgc, S_TG)
    for k in range(rw):
        cols = slice(k * C, (k + 1) * C)
        tg_out[:, cols] = (fz[:, cols] + tgc[k].astype(F32)).astype(BF)

    got(lrt, S_LRR)
    doubled(lrt)
    spread([slot_id(j, yy) for yy in range(ny)])
    vcs[...] = (
        jnp.dot(mt[:, : ny * R], ug[...].reshape(ny * R, C), preferred_element_type=F32)
        .astype(BF)
        .reshape(rw, T, C)
    )
    row_exchange(lambda q: vcs.at[q], vc.at[j], S_VC)
    of = slw[0:1, :]
    lr = lrt[...].astype(F32)
    for yy in range(ny):
        mbig[yy * R : (yy + 1) * R, :] = jnp.where(of == slot_id(j, yy), lr, 0.0).astype(BF)
    pbs[...] = (
        jnp.dot(mbig[: ny * R, :], dyr[...].reshape(rw * T, C), preferred_element_type=F32)
        .astype(BF)
        .reshape(ny, R, C)
    )
    y_exchange(lambda q: pbs.at[q], gbp.at[y], S_GB)

    got(bz, S_BZ)
    got(vc, S_VC)
    v_out[...] = (sum_of(bz, nz) + sum_of(vc, rw)).astype(BF)
    got(gbp, S_GB)
    gb_out[...] = sum_of(gbp, ny)
    got(ga_out, S_GA)

    def sent(ref, stage):
        pltpu.make_async_copy(ref, ref, ss.at[stage]).wait()

    row = pl.ds(0, rw - 1)
    sent(dg.at[0, row], S_DT)
    sent(dyr.at[row], S_DY)
    sent(slw.at[:, pl.ds(0, (rw - 1) * 128)], S_SL)
    sent(xr.at[row], S_X)
    sent(dyf.at[:, pl.ds(0, (nz - 1) * 128)], S_DYZ)
    sent(ug.at[pl.ds(0, ny - 1)], S_U)
    sent(lgp.at[row], S_LGP)
    sent(lgz.at[pl.ds(0, nz - 1)], S_LGZ)
    sent(lgt.at[:, pl.ds(0, (rw - 1) * 128)], S_LGR)
    sent(bz.at[pl.ds(0, nz - 1)], S_BZ)
    sent(lrp.at[row], S_LRP)
    sent(lrz.at[pl.ds(0, nz - 1)], S_LRZ)
    sent(lrt.at[:, pl.ds(0, (rw - 1) * 128)], S_LRR)
    sent(tgc.at[row], S_TG)
    sent(vc.at[row], S_VC)
    sent(gbp.at[pl.ds(0, ny - 1)], S_GB)
    sent(fin.at[row], S_GA)
    for d in range(2):
        for h in range(2):
            for s in range(1, ring_steps(ny, d, h) + 1):
                ag_copy(d, h, s).wait_send()
                rs_copy(d, h, s).wait_send()


def shards(nx, ny, nz, tokens, weight, down, up, dy, adapter, lengths, table):
    rw = 2 * nx
    f = rw * C
    steps = max(1, ny // 2)
    hr = rw // 2 * R
    vm = pltpu.VMEM
    anywhere = pl.BlockSpec(memory_space=pl.ANY)
    vmem = pl.BlockSpec(memory_space=pltpu.VMEM)
    smem = pl.BlockSpec(memory_space=pltpu.SMEM)
    values, token_grad, grad_a, grad_b = pl.pallas_call(
        functools.partial(kernel, nx, ny, nz),
        out_shape=(
            jax.ShapeDtypeStruct((T, C), BF),
            jax.ShapeDtypeStruct((T, f), BF),
            jax.ShapeDtypeStruct((R, f), F32),
            jax.ShapeDtypeStruct((R, C), F32),
        ),
        in_specs=[anywhere] * 5 + [smem] * 3,
        out_specs=(vmem, vmem, vmem, vmem),
        scratch_shapes=[
            vm((T, f), BF),
            vm((f, nz * C), BF),
            vm((rw, T, C), BF),
            vm((ny, rw, R, C), BF),
            vm((rw, T, C), BF),
            vm((8, rw * T), jnp.int32),
            vm((8, T), jnp.int32),
            vm((T, nz * C), BF),
            vm((ny, R, C), BF),
            vm((rw, R, T), BF),
            vm((rw, R, T), BF),
            vm((R, T), BF),
            vm((nz, R, T), BF),
            vm((R, T), BF),
            vm((R, rw * T), BF),
            vm((nz, T, C), BF),
            vm((nz, T, C), BF),
            vm((T, f), F32),
            vm((rw, R, T), F32),
            vm((rw, R, T), BF),
            vm((rw, R, T), BF),
            vm((R, T), BF),
            vm((nz, R, T), BF),
            vm((R, T), BF),
            vm((R, rw * T), BF),
            vm((max(rw, ny) * R, rw * T), BF),
            vm((rw * T, max(rw, ny) * R), BF),
            vm((rw * T, 128), F32),
            vm((rw * T, 128), F32),
            vm((rw * T, C), F32),
            vm((rw, T, C), BF),
            vm((rw, T, C), BF),
            vm((rw, T, C), BF),
            vm((rw, T, C), BF),
            vm((ny, R, C), BF),
            vm((ny, R, C), BF),
            vm((ny, rw * R, C), F32),
            vm((ny, rw * R, C), BF),
            vm((2, 2, steps, hr, C), BF),
            vm((rw, R, C), F32),
            pltpu.SemaphoreType.DMA((N_STAGES,)),
            pltpu.SemaphoreType.DMA((N_STAGES,)),
            pltpu.SemaphoreType.DMA((2, 2, steps)),
            pltpu.SemaphoreType.DMA((2, 2, steps)),
            pltpu.SemaphoreType.DMA((2, 2, steps)),
            pltpu.SemaphoreType.DMA((2, 2, steps)),
            pltpu.SemaphoreType.DMA((2,)),
        ],
        compiler_params=pltpu.CompilerParams(
            collective_id=0, has_side_effects=True, vmem_limit_bytes=48 * 1024 * 1024
        ),
    )(
        tokens,
        weight,
        jnp.swapaxes(down[0], 0, 1),
        up[0],
        dy,
        adapter.reshape(-1),
        lengths.reshape(-1),
        table,
    )
    return values, token_grad, jnp.swapaxes(grad_a, 0, 1)[None], grad_b[None]


def solution(mesh, nx=4):
    dp, nz = mesh.shape["dp"], mesh.shape["tensor"]
    return jax.shard_map(
        functools.partial(shards, nx, dp // (2 * nx), nz),
        mesh=mesh,
        in_specs=(
            P("dp", "tensor"),
            P("tensor", None),
            P("dp", "tensor", None),
            P("dp", None, "tensor"),
            P("dp", "tensor"),
            P("dp", None),
            P("dp", None),
            P(),
        ),
        out_specs=(
            P("dp", "tensor"),
            P("dp", "tensor"),
            P("dp", "tensor", None),
            P("dp", None, "tensor"),
        ),
        check_vma=False,
    )
```

time: 383 us -> 97.1 us (0.25)
  waiting for transfers between devices: 192 us -> 0 us
  Pallas kernels: 0 us -> 86.5 us
  blocking collectives: 79.7 us -> 0 us
  matrix products: 30.7 us -> 0 us
  starting transfers between devices: 30.3 us -> 0 us
  local copies, waits for them, and re-layouts: 25.2 us -> 9.51 us
  between operations: 14.6 us -> 0.66 us
  other arithmetic: 9.58 us -> 0 us
    all_gather x1 -> x0, waiting for transfers between devices: 115 us -> none  [shards(): piece = lax.all_gather(own_panels, 'dp', axis=0, tiled=True)]
    pallas_call x0 -> x1, Pallas kernels: none -> 86.5 us  [shards(): pl.pallas_call(functools.partial(kernel, nx, ny, nz), out_shape=(jax.Shap...]
    psum x1 -> x0, waiting for transfers between devices: 70.3 us -> none  [shards(): down_total, backward_total = lax.psum((down_part, back_part), 'tensor')]
    unnamed x1 -> x0, blocking collectives: 61.1 us -> none
    dot_general x10 -> x0, matrix products: 30.7 us -> none  [the longest x1 16.3 us: shards(): jnp.dot(select, piece, preferred_element_type=jnp.float32)]
    all_to_all x2 -> x0, starting transfers between devices: 30.2 us -> none  [the longest x1 15.1 us: shards(): lax.all_to_all(seg_grads.reshape(seq_count, groups, piece_len), 'dp', spl...]
    all_gather x1 -> x0, blocking collectives: 18.6 us -> none  [shards(): lax.all_gather(output_gradient, 'tensor', axis=1, tiled=True)]
    reshape x9 -> x0, local copies, waits for them, and re-layouts: 17.9 us -> none  [the longest x2 5.67 us: shards(): fetched[:, :down_panel_count].reshape(seq_count, local_width, rank_extent)]
  transfers between devices with their start and end apart: 5 -> 0, of which waited for: 3 -> 0; matrix products, arithmetic and copies ran while one was open for 4% -> 0% of each run, Pallas kernels for 0% -> 0%
where the time goes in v1:
time: 97.1 us; the launch traced here: 96.7 us
  Pallas kernels  86.5 us (89%)
  local copies, waits for them, and re-layouts  9.51 us (10%)
    pallas_call x1, Pallas kernels, shards(): pl.pallas_call(functools.partial(kernel, nx, ny, nz), out_shape=(jax.Shap...  86.5 us
    unnamed x20, local copies, waits for them, and re-layouts  9.51 us

profile of v1, /device:TPU:1, one launch (start us, length us, event | category | flops | bytes accessed | tf_op | source)
XLA Modules:
  0.0 96.7 jit_solution(13650719618626565333)
XLA Ops:
  0.6 0.0 copy-start
  0.6 1.6 %copy-done = bf16[1024,1024]{1,0:T(8,128)(2,1)S(1)} copy-done((bf16[1024,1024]{1,0:T(8,128)(2,1)S(1)}, bf16[1024,1024]{1,0:T(8,128)(2,1)}, u32[]{:S(2)}) %copy-start) | copy-done | bytes 2097176
  2.2 0.0 copy-start.1
  2.2 0.9 copy-done.1
  3.2 0.0 copy-start.2
  3.2 0.9 copy-done.2
  4.1 0.0 copy-start.3
  4.1 0.8 copy-done.3
  4.8 0.0 copy-start.4
  4.8 0.7 copy-done.4
  5.6 0.0 copy-start.5
  5.6 0.7 copy-done.5
  6.2 0.0 copy-start.6
  6.2 0.7 copy-done.6
  6.9 0.0 copy-start.7
  6.9 0.7 copy-done.7
  7.5 86.5 %shard_map.111 = (bf16[128,128]{1,0:T(8,128)(2,1)S(1)}, bf16[128,1024]{1,0:T(8,128)(2,1)S(1)}, f32[64,1024]{1,0:T(8,128)S(1)}, f32[64,128]{1,0:T(8,128)S(1)}) custom-call(bf16[128,1024]{1,0:T(8,128)(2,1)S(1)} %copy-done.1, bf16[1024,1024]{1,0:T(8,128)(2,1)S(1)} %copy-done, bf16[64,1024]{1,0:T(8,128)(2,1)S(1)} %bitcast.11, bf16[64,128]{1,0:T(8,128)(2,1)S(1)} %bitcast.13, ...), custom_call_target="tpu_custom_call" | custom-call | tf_op jit(solution)/shard_map/pallas_call | solution.py:421
  94.1 0.6 copy.16
  94.7 0.7 copy.17
  95.4 0.7 copy.18
  96.1 0.6 copy.19
Async XLA Ops:
  0.6 1.6 %copy-start = (bf16[1024,1024]{1,0:T(8,128)(2,1)S(1)}, bf16[1024,1024]{1,0:T(8,128)(2,1)}, u32[]{:S(2)}) copy-start(bf16[1024,1024]{1,0:T(8,128)(2,1)} %w_hbm.1) | copy-start | bytes 6291460
  2.2 0.9 copy-start.1
  3.2 0.9 copy-start.2
  4.1 0.8 copy-start.3
  4.8 0.7 copy-start.4
  5.6 0.7 copy-start.5
  6.2 0.7 copy-start.6
  6.9 0.7 copy-start.7

commit v2 on v1

v2 whole, which is shorter than its diff:
```python
import functools

import jax
import jax.numpy as jnp
from jax import lax
from jax.experimental import pallas as pl
from jax.experimental.pallas import tpu as pltpu
from jax.sharding import PartitionSpec as P

LIMIT = 56 * 1024 * 1024
MESH = pl.DeviceIdType.MESH
BF = jnp.bfloat16
F32 = jnp.float32
NT = (((1,), (1,)), ((), ()))
T = 128
R = 64
C = 128

(S_DT, S_DY, S_SL, S_X, S_DYZ, S_U, S_LGP, S_LGZ, S_LGR, S_BZ, S_LRP, S_LRZ, S_LRR, S_TG, S_VC, S_GB, S_GA) = range(17)
N_STAGES = 17


def ring_steps(ny, d, h):
    return ny // 2 if d == h else ny - 1 - ny // 2


def kernel(
    nx, ny, nz,
    x_hbm, w_hbm, dt_hbm, u_hbm, dy_hbm, adp, lens, tab,
    v_out, tg_out, ga_out, gb_out,
    xv, wv, xr, dg, dyr, slw, slo, dyf, ug,
    lgps, lgp, lgzs, lgz, lgs, lgt,
    bs, bz, fz,
    lracc, lrps, lrp, lrzs, lrz, lrs, lrt,
    mbig, mt, two, st, tgacc, tgs, tgc, vcs, vc, pbs, gbp,
    pa, pas, rb, fin,
    ss, rs, ag_s, ag_r, rs_s, rs_r, ld,
):
    rw = 2 * nx
    hw = rw // 2
    me = lax.axis_index("dp")
    z = lax.axis_index("tensor")
    c = me % 2
    y = (me // 2) % ny
    x = me // (2 * ny)
    j = x * 2 + c

    def row_dev(jj):
        odd = lax.rem(jj, 2)
        return ny * (jj - odd) + odd + 2 * y

    def y_dev(yy):
        return x * (2 * ny) + yy * 2 + c

    def slot_id(jj, yy):
        return (jj // 2) * (2 * ny) + yy * 2 + jj % 2

    def col(i):
        return pl.ds(pl.multiple_of(i * 128, 128), 128)

    row = pl.ds(0, rw - 1)
    row_cols = pl.ds(0, (rw - 1) * 128)
    zs = pl.ds(0, nz - 1)
    ys = pl.ds(0, ny - 1)
    arrives = {
        S_DT: (dg.at[y], dg.at[0, row]),
        S_DY: (dyr, dyr.at[row]),
        S_SL: (slw, slw.at[:, row_cols]),
        S_X: (xr, xr.at[row]),
        S_DYZ: (dyf, dyf.at[:, pl.ds(0, (nz - 1) * 128)]),
        S_U: (ug, ug.at[ys]),
        S_LGP: (lgp, lgp.at[row]),
        S_LGZ: (lgz, lgz.at[zs]),
        S_LGR: (lgt, lgt.at[:, row_cols]),
        S_BZ: (bz, bz.at[zs]),
        S_LRP: (lrp, lrp.at[row]),
        S_LRZ: (lrz, lrz.at[zs]),
        S_LRR: (lrt, lrt.at[:, row_cols]),
        S_TG: (tgc, tgc.at[row]),
        S_VC: (vc, vc.at[row]),
        S_GB: (gbp, gbp.at[ys]),
        S_GA: (ga_out, fin.at[row]),
    }
    started, done = [], []

    def rcopy(src, dst, s, r, dev):
        return pltpu.make_async_remote_copy(
            src_ref=src, dst_ref=dst, send_sem=s, recv_sem=r, device_id=dev, device_id_type=MESH
        )

    def exchange(n, mine, dev, src, dst, stage):
        @pl.loop(1, n)
        def _(i):
            q = lax.rem(mine + i, n)
            rcopy(src(q), dst, ss.at[stage], rs.at[stage], dev(q)).start()

        pltpu.make_async_copy(src(mine), dst, rs.at[stage]).start()
        started.append(stage)

    def row_exchange(src, dst, stage):
        exchange(rw, j, lambda q: (row_dev(q), z), src, dst, stage)

    def y_exchange(src, dst, stage):
        exchange(ny, y, lambda q: (y_dev(q), z), src, dst, stage)

    def z_exchange(src, dst, stage):
        exchange(nz, z, lambda q: (me, q), src, dst, stage)

    def got(stage):
        ref = arrives[stage][0]
        pltpu.make_async_copy(ref, ref, rs.at[stage]).wait()
        done.append(stage)

    barrier = pltpu.get_barrier_semaphore()

    @pl.loop(1, rw)
    def _(i):
        pl.semaphore_signal(barrier, inc=1, device_id=(row_dev((j + i) % rw), z), device_id_type=MESH)

    @pl.loop(1, ny)
    def _(i):
        pl.semaphore_signal(barrier, inc=1, device_id=(y_dev((y + i) % ny), z), device_id_type=MESH)

    @pl.loop(1, nz)
    def _(i):
        pl.semaphore_signal(barrier, inc=1, device_id=(me, (z + i) % nz), device_id_type=MESH)

    load_w = pltpu.make_async_copy(w_hbm, wv, ld.at[0])
    load_x = pltpu.make_async_copy(x_hbm, xv, ld.at[1])
    load_x.start()
    load_w.start()

    position = lax.broadcasted_iota(jnp.int32, (8, T), 1)
    slots = jnp.full((8, T), 0, jnp.int32)
    begin = jnp.int32(0)
    for k in range(8):
        slots = jnp.where(position >= begin, tab[adp[k]], slots)
        begin = begin + lens[k]
    slo[...] = slots

    def work():
        pl.semaphore_wait(barrier, rw + ny + nz - 3)

        row_exchange(lambda q: dt_hbm.at[:, col(q)], dg.at[y, j], S_DT)
        y_exchange(lambda q: u_hbm, ug.at[y], S_U)
        row_exchange(lambda q: slo, slw.at[:, col(j)], S_SL)
        row_exchange(lambda q: dy_hbm, dyr.at[j], S_DY)
        z_exchange(lambda q: dy_hbm, dyf.at[:, col(z)], S_DYZ)
        row_exchange(lambda q: x_hbm.at[:, col(q)], xr.at[j], S_X)

        def half(h):
            return pl.ds(h * hw, hw)

        def ag_copy(d, h, s):
            yy = (y - (s - 1) if d == 0 else y + (s - 1)) % ny
            to = (y + 1 if d == 0 else y - 1) % ny
            block = dg.at[yy, half(h)]
            return rcopy(block, block, ag_s.at[d, h, s - 1], ag_r.at[d, h, s - 1], (y_dev(to), z))

        def ag_send(s):
            for h in range(2):
                for d in range(2):
                    if s <= ring_steps(ny, d, h):
                        started.append((ag_copy, d, h, s))
                        ag_copy(d, h, s).start()

        def ag_got(s):
            for h in range(2):
                for d in range(2):
                    if s <= ring_steps(ny, d, h):
                        ag_copy(d, h, s).wait_recv()
                        done.append((ag_copy, d, h, s))
                        if s + 1 <= ring_steps(ny, d, h):
                            started.append((ag_copy, d, h, s + 1))
                            ag_copy(d, h, s + 1).start()

        def sum_of(ref, n):
            total = ref[0].astype(F32)
            for i in range(1, n):
                total = total + ref[i].astype(F32)
            return total

        def low_rank_chunk(yy):
            panels = dg[yy].reshape(rw * R, C)

            @pl.loop(0, rw // 2)
            def _(i):
                pair = xr[pl.ds(2 * i, 2)].reshape(2 * T, C)
                wide = lax.dot_general(panels, pair, NT, preferred_element_type=F32)
                for e in range(2):
                    of = slw[0:1, col(2 * i + e)]
                    total = lracc[2 * i + e]
                    for k in range(rw):
                        total = total + jnp.where(
                            of == slot_id(k, yy), wide[k * R : (k + 1) * R, e * T : (e + 1) * T], 0.0
                        )
                    lracc[2 * i + e] = total

        def grad_chunk(yy):
            of = slw[0:1, :]
            lg = lgt[...].astype(F32)
            for k in range(rw):
                mbig[k * R : (k + 1) * R, :] = jnp.where(of == slot_id(k, yy), lg, 0.0).astype(BF)
            pa[yy] = jnp.dot(mbig[: rw * R, :], xr[...].reshape(rw * T, C), preferred_element_type=F32)

        def hrows(h):
            return pl.ds(h * hw * R, hw * R)

        def rs_copy(d, h, s):
            n = ring_steps(ny, d, h)
            dest = (y + (n - s + 1) if d == 0 else y - (n - s + 1)) % ny
            to = (y + 1 if d == 0 else y - 1) % ny
            return rcopy(
                pas.at[dest, hrows(h)], rb.at[d, h, s - 1], rs_s.at[d, h, s - 1], rs_r.at[d, h, s - 1], (y_dev(to), z)
            )

        def rs_send(d, h, s):
            n = ring_steps(ny, d, h)
            if s > n:
                return
            dest = (y + (n - s + 1) if d == 0 else y - (n - s + 1)) % ny
            part = pa[dest, hrows(h)]
            if s > 1:
                rs_got(d, h, s - 1)
                part = part + rb[d, h, s - 2].astype(F32)
            pas[dest, hrows(h)] = part.astype(BF)
            started.append((rs_copy, d, h, s))
            rs_copy(d, h, s).start()

        def rs_got(d, h, s):
            rs_copy(d, h, s).wait_recv()
            done.append((rs_copy, d, h, s))

        far = ny // 2

        def rs_step(s):
            for d in range(2):
                rs_send(d, d, s)
            for d in range(2):
                rs_send(d, 1 - d, s)

        def both(step, distance):
            step((y + distance) % ny)
            step((y - distance) % ny)

        lane = lax.broadcasted_iota(jnp.int32, (T, 128), 1)

        def rows_of(b):
            return pl.ds(pl.multiple_of(b * T, T), T)

        def doubled(src):
            @pl.loop(0, rw)
            def _(b):
                one = src[:, col(b)].astype(F32)
                two[rows_of(b), :] = jnp.concatenate([one, one], axis=0).T

        def spread(ids):
            @pl.loop(0, rw)
            def _(b):
                of = st[rows_of(b), :]
                rows = two[rows_of(b), :]
                for m in range(len(ids) // 2):
                    want = jnp.where(lane < R, ids[2 * m], ids[2 * m + 1]).astype(F32)
                    mt[rows_of(b), m * 128 : (m + 1) * 128] = jnp.where(of == want, rows, 0.0).astype(BF)

        load_x.wait()
        load_w.wait()

        @pl.loop(0, nz // 2)
        def _(i):
            part = jnp.dot(
                xv[...], wv[:, pl.ds(pl.multiple_of(i * 256, 256), 256)], preferred_element_type=F32
            ).astype(BF)
            bs[2 * i] = part[:, :C]
            bs[2 * i + 1] = part[:, C:]

        got(S_DT)
        ag_send(1)

        got(S_U)
        got(S_SL)
        got(S_DY)

        @pl.loop(0, rw)
        def _(b):
            wide = lax.dot_general(
                ug[...].reshape(ny * R, C), dyr[b], NT, preferred_element_type=F32
            )
            of = slw[0:1, col(b)]
            total = jnp.zeros((R, T), F32)
            for yy in range(ny):
                total = total + jnp.where(of == slot_id(j, yy), wide[yy * R : (yy + 1) * R], 0.0)
            lgps[b] = total.astype(BF)

        row_exchange(lambda q: lgps.at[q], lgp.at[j], S_LGP)

        @pl.loop(0, rw)
        def _(b):
            of = jnp.broadcast_to(slw[0:1, col(b)].astype(F32), (T, T))
            st[pl.ds(pl.multiple_of(b * T, T), T), :] = of.T
            lracc[b] = jnp.zeros((R, T), F32)

        ag_got(1)
        got(S_LGP)
        lgzs[...] = sum_of(lgp, rw).astype(BF)
        z_exchange(lambda q: lgzs, lgz.at[z], S_LGZ)

        got(S_X)
        low_rank_chunk(y)
        if far > 1:
            ag_got(2)

        got(S_LGZ)
        lgs[...] = (2.0 * sum_of(lgz, nz)).astype(BF)
        row_exchange(lambda q: lgs, lgt.at[:, col(j)], S_LGR)
        z_exchange(lambda q: bs.at[q], bz.at[z], S_BZ)

        if far > 1:
            both(low_rank_chunk, 1)
        if far > 2:
            ag_got(3)

        got(S_DYZ)

        @pl.loop(0, rw // 2)
        def _(i):
            f = pl.ds(pl.multiple_of(i * 256, 256), 256)
            fz[:, f] = lax.dot_general(dyf[...], wv[f, :], NT, preferred_element_type=F32)

        got(S_LGR)
        grad_chunk((y + far) % ny)
        for d in range(2):
            rs_send(d, d, 1)
        if far > 1:
            both(grad_chunk, far - 1)
            for d in range(2):
                rs_send(d, 1 - d, 1)
        for s in range(4, far + 1):
            ag_got(s)
        for s in range(2, far):
            both(low_rank_chunk, s)
        low_rank_chunk((y + far) % ny)

        @pl.loop(0, rw)
        def _(b):
            lrps[b] = lracc[b].astype(BF)

        row_exchange(lambda q: lrps.at[q], lrp.at[j], S_LRP)

        for s in range(2, far):
            both(grad_chunk, far - s)
        if far > 1:
            rs_step(2)
        doubled(lgt)
        grad_chunk(y)

        got(S_LRP)
        lrzs[...] = sum_of(lrp, rw).astype(BF)
        z_exchange(lambda q: lrzs, lrz.at[z], S_LRZ)

        if far > 2:
            rs_step(3)
        tgacc[...] = jnp.zeros_like(tgacc)

        @pl.loop(0, ny)
        def _(yy):
            spread([slot_id(k, yy) for k in range(rw)])
            tgacc[...] += jnp.dot(
                mt[:, : rw * R], dg[yy].reshape(rw * R, C), preferred_element_type=F32
            )

        tgs[...] = tgacc[...].astype(BF).reshape(rw, T, C)
        row_exchange(lambda q: tgs.at[q], tgc.at[j], S_TG)

        got(S_LRZ)
        lrs[...] = (2.0 * sum_of(lrz, nz)).astype(BF)
        row_exchange(lambda q: lrs, lrt.at[:, col(j)], S_LRR)

        for s in range(4, far + 1):
            rs_step(s)
        for h in range(2):
            total = pa[y, hrows(h)]
            for d in range(2):
                n = ring_steps(ny, d, h)
                if n > 0:
                    rs_got(d, h, n)
                    total = total + rb[d, h, n - 1].astype(F32)
            for k in range(hw):
                fin[h * hw + k] = total[k * R : (k + 1) * R]
        row_exchange(lambda q: fin.at[q], ga_out.at[:, col(j)], S_GA)

        got(S_LRR)
        of = slw[0:1, :]
        lr = lrt[...].astype(F32)
        for yy in range(ny):
            mbig[yy * R : (yy + 1) * R, :] = jnp.where(of == slot_id(j, yy), lr, 0.0).astype(BF)
        pbs[...] = (
            jnp.dot(mbig[: ny * R, :], dyr[...].reshape(rw * T, C), preferred_element_type=F32)
            .astype(BF)
            .reshape(ny, R, C)
        )
        y_exchange(lambda q: pbs.at[q], gbp.at[y], S_GB)
        doubled(lrt)
        spread([slot_id(j, yy) for yy in range(ny)])
        vcs[...] = (
            jnp.dot(mt[:, : ny * R], ug[...].reshape(ny * R, C), preferred_element_type=F32)
            .astype(BF)
            .reshape(rw, T, C)
        )
        row_exchange(lambda q: vcs.at[q], vc.at[j], S_VC)

        got(S_TG)
        for k in range(rw):
            cols = slice(k * C, (k + 1) * C)
            tg_out[:, cols] = (fz[:, cols] + tgc[k].astype(F32)).astype(BF)
        got(S_BZ)
        got(S_VC)
        v_out[...] = (sum_of(bz, nz) + sum_of(vc, rw)).astype(BF)
        got(S_GB)
        gb_out[...] = sum_of(gbp, ny)
        got(S_GA)

    work()

    for one in started:
        if isinstance(one, tuple):
            if one not in done:
                one[0](*one[1:]).wait_recv()
            one[0](*one[1:]).wait_send()
        else:
            if one not in done:
                got(one)
            ref = arrives[one][1]
            pltpu.make_async_copy(ref, ref, ss.at[one]).wait()


def shards(nx, ny, nz, tokens, weight, down, up, dy, adapter, lengths, table):
    rw = 2 * nx
    f = rw * C
    steps = max(1, ny // 2)
    hr = rw // 2 * R
    vm = pltpu.VMEM
    anywhere = pl.BlockSpec(memory_space=pl.ANY)
    vmem = pl.BlockSpec(memory_space=pltpu.VMEM)
    smem = pl.BlockSpec(memory_space=pltpu.SMEM)
    values, token_grad, grad_a, grad_b = pl.pallas_call(
        functools.partial(kernel, nx, ny, nz),
        out_shape=(
            jax.ShapeDtypeStruct((T, C), BF),
            jax.ShapeDtypeStruct((T, f), BF),
            jax.ShapeDtypeStruct((R, f), F32),
            jax.ShapeDtypeStruct((R, C), F32),
        ),
        in_specs=[anywhere] * 5 + [smem] * 3,
        out_specs=(vmem, vmem, vmem, vmem),
        scratch_shapes=[
            vm((T, f), BF),
            vm((f, nz * C), BF),
            vm((rw, T, C), BF),
            vm((ny, rw, R, C), BF),
            vm((rw, T, C), BF),
            vm((8, rw * T), jnp.int32),
            vm((8, T), jnp.int32),
            vm((T, nz * C), BF),
            vm((ny, R, C), BF),
            vm((rw, R, T), BF),
            vm((rw, R, T), BF),
            vm((R, T), BF),
            vm((nz, R, T), BF),
            vm((R, T), BF),
            vm((R, rw * T), BF),
            vm((nz, T, C), BF),
            vm((nz, T, C), BF),
            vm((T, f), F32),
            vm((rw, R, T), F32),
            vm((rw, R, T), BF),
            vm((rw, R, T), BF),
            vm((R, T), BF),
            vm((nz, R, T), BF),
            vm((R, T), BF),
            vm((R, rw * T), BF),
            vm((max(rw, ny) * R, rw * T), BF),
            vm((rw * T, max(rw, ny) * R), BF),
            vm((rw * T, 128), F32),
            vm((rw * T, 128), F32),
            vm((rw * T, C), F32),
            vm((rw, T, C), BF),
            vm((rw, T, C), BF),
            vm((rw, T, C), BF),
            vm((rw, T, C), BF),
            vm((ny, R, C), BF),
            vm((ny, R, C), BF),
            vm((ny, rw * R, C), F32),
            vm((ny, rw * R, C), BF),
            vm((2, 2, steps, hr, C), BF),
            vm((rw, R, C), F32),
            pltpu.SemaphoreType.DMA((N_STAGES,)),
            pltpu.SemaphoreType.DMA((N_STAGES,)),
            pltpu.SemaphoreType.DMA((2, 2, steps)),
            pltpu.SemaphoreType.DMA((2, 2, steps)),
            pltpu.SemaphoreType.DMA((2, 2, steps)),
            pltpu.SemaphoreType.DMA((2, 2, steps)),
            pltpu.SemaphoreType.DMA((2,)),
        ],
        compiler_params=pltpu.CompilerParams(
            collective_id=0, has_side_effects=True, vmem_limit_bytes=LIMIT
        ),
    )(
        tokens,
        weight,
        jnp.swapaxes(down[0], 0, 1),
        up[0],
        dy,
        adapter.reshape(-1),
        lengths.reshape(-1),
        table,
    )
    return values, token_grad, jnp.swapaxes(grad_a, 0, 1)[None], grad_b[None]


def solution(mesh, nx=4):
    dp, nz = mesh.shape["dp"], mesh.shape["tensor"]
    return jax.shard_map(
        functools.partial(shards, nx, dp // (2 * nx), nz),
        mesh=mesh,
        in_specs=(
            P("dp", "tensor"),
            P("tensor", None),
            P("dp", "tensor", None),
            P("dp", None, "tensor"),
            P("dp", "tensor"),
            P("dp", None),
            P("dp", None),
            P(),
        ),
        out_specs=(
            P("dp", "tensor"),
            P("dp", "tensor"),
            P("dp", "tensor", None),
            P("dp", None, "tensor"),
        ),
        check_vma=False,
    )
```

time: 97.1 us -> 81.6 us (0.84)
  Pallas kernels: 86.5 us -> 74.6 us
  local copies, waits for them, and re-layouts: 9.51 us -> 6.09 us
    pallas_call x1, Pallas kernels: 86.5 us -> 74.6 us  [shards(): pl.pallas_call(functools.partial(kernel, nx, ny, nz), out_shape=(jax.Shap...]
    unnamed x20 -> x4, local copies, waits for them, and re-layouts: 9.51 us -> 6.09 us
where the time goes in v2:
time: 81.6 us; the launch traced here: 81.3 us
  Pallas kernels  74.6 us (91%)
  local copies, waits for them, and re-layouts  6.09 us (7%)
    pallas_call x1, Pallas kernels, shards(): pl.pallas_call(functools.partial(kernel, nx, ny, nz), out_shape=(jax.Shap...  74.6 us
    unnamed x4, local copies, waits for them, and re-layouts  6.09 us

profile of v2, /device:TPU:1, one launch (start us, length us, event | category | flops | bytes accessed | tf_op | source)
XLA Modules:
  0.0 81.3 jit_solution(16835656569700940142)
XLA Ops:
  0.6 74.6 %shard_map.111 = (bf16[128,128]{1,0:T(8,128)(2,1)}, bf16[128,1024]{1,0:T(8,128)(2,1)}, f32[64,1024]{1,0:T(8,128)}, f32[64,128]{1,0:T(8,128)}) custom-call(bf16[128,1024]{1,0:T(8,128)(2,1)} %x_hbm.1, bf16[1024,1024]{1,0:T(8,128)(2,1)} %w_hbm.1, bf16[64,1024]{1,0:T(8,128)(2,1)} %bitcast.11, bf16[64,128]{1,0:T(8,128)(2,1)} %bitcast.13, ...), custom_call_target="tpu_custom_call" | custom-call | tf_op jit(solution)/shard_map/pallas_call | solution.py:446
  75.2 1.4 %copy.16 = bf16[128,128]{1,0:T(8,128)(2,1)} copy(bf16[128,128]{1,0:T(8,128)(2,1)} %get-tuple-element.16) | data formatting | bytes 65536
  76.6 1.7 %copy.17 = bf16[128,1024]{1,0:T(8,128)(2,1)} copy(bf16[128,1024]{1,0:T(8,128)(2,1)} %get-tuple-element.17) | data formatting | bytes 524288
  78.3 1.7 %copy.18 = f32[1,1024,64]{1,2,0:T(8,128)} copy(f32[1,1024,64]{1,2,0:T(8,128)} %bitcast.10) | data formatting | bytes 524288
  79.9 1.4 %copy.19 = f32[1,64,128]{2,1,0:T(8,128)} copy(f32[1,64,128]{2,1,0:T(8,128)} %bitcast.12) | data formatting | bytes 65536

commit v3 on v2

--- a/solution.py
+++ b/solution.py
@@ -33,7 +33,7 @@
     bs, bz, fz,
     lracc, lrps, lrp, lrzs, lrz, lrs, lrt,
     mbig, mt, two, st, tgacc, tgs, tgc, vcs, vc, pbs, gbp,
-    pa, pas, rb, fin,
+    pa, pas, rb, fin, gar,
     ss, rs, ag_s, ag_r, rs_s, rs_r, ld,
 ):
     rw = 2 * nx
@@ -79,7 +79,7 @@
         S_TG: (tgc, tgc.at[row]),
         S_VC: (vc, vc.at[row]),
         S_GB: (gbp, gbp.at[ys]),
-        S_GA: (ga_out, fin.at[row]),
+        S_GA: (gar, fin.at[row]),
     }
     started, done = [], []
 
@@ -309,16 +309,7 @@
         low_rank_chunk(y)
         if far > 1:
             ag_got(2)
-
-        got(S_LGZ)
-        lgs[...] = (2.0 * sum_of(lgz, nz)).astype(BF)
-        row_exchange(lambda q: lgs, lgt.at[:, col(j)], S_LGR)
-        z_exchange(lambda q: bs.at[q], bz.at[z], S_BZ)
-
-        if far > 1:
             both(low_rank_chunk, 1)
-        if far > 2:
-            ag_got(3)
 
         got(S_DYZ)
 
@@ -326,6 +317,27 @@
         def _(i):
             f = pl.ds(pl.multiple_of(i * 256, 256), 256)
             fz[:, f] = lax.dot_general(dyf[...], wv[f, :], NT, preferred_element_type=F32)
+
+        if far > 2:
+            ag_got(3)
+        if far > 2:
+            both(low_rank_chunk, 2)
+
+        got(S_LGZ)
+        lgs[...] = (2.0 * sum_of(lgz, nz)).astype(BF)
+        row_exchange(lambda q: lgs, lgt.at[:, col(j)], S_LGR)
+
+        for s in range(4, far + 1):
+            ag_got(s)
+        for s in range(3, far):
+            both(low_rank_chunk, s)
+        low_rank_chunk((y + far) % ny)
+
+        @pl.loop(0, rw)
+        def _(b):
+            lrps[b] = lracc[b].astype(BF)
+
+        row_exchange(lambda q: lrps.at[q], lrp.at[j], S_LRP)
 
         got(S_LGR)
         grad_chunk((y + far) % ny)
@@ -335,31 +347,17 @@
             both(grad_chunk, far - 1)
             for d in range(2):
                 rs_send(d, 1 - d, 1)
-        for s in range(4, far + 1):
-            ag_got(s)
-        for s in range(2, far):
-            both(low_rank_chunk, s)
-        low_rank_chunk((y + far) % ny)
-
-        @pl.loop(0, rw)
-        def _(b):
-            lrps[b] = lracc[b].astype(BF)
-
-        row_exchange(lambda q: lrps.at[q], lrp.at[j], S_LRP)
+
+        got(S_LRP)
+        lrzs[...] = sum_of(lrp, rw).astype(BF)
+        z_exchange(lambda q: lrzs, lrz.at[z], S_LRZ)
+        z_exchange(lambda q: bs.at[q], bz.at[z], S_BZ)
 
         for s in range(2, far):
             both(grad_chunk, far - s)
         if far > 1:
             rs_step(2)
         doubled(lgt)
-        grad_chunk(y)
-
-        got(S_LRP)
-        lrzs[...] = sum_of(lrp, rw).astype(BF)
-        z_exchange(lambda q: lrzs, lrz.at[z], S_LRZ)
-
-        if far > 2:
-            rs_step(3)
         tgacc[...] = jnp.zeros_like(tgacc)
 
         @pl.loop(0, ny)
@@ -371,23 +369,15 @@
 
         tgs[...] = tgacc[...].astype(BF).reshape(rw, T, C)
         row_exchange(lambda q: tgs.at[q], tgc.at[j], S_TG)
+        if far > 2:
+            rs_step(3)
+        grad_chunk(y)
 
         got(S_LRZ)
         lrs[...] = (2.0 * sum_of(lrz, nz)).astype(BF)
         row_exchange(lambda q: lrs, lrt.at[:, col(j)], S_LRR)
-
         for s in range(4, far + 1):
             rs_step(s)
-        for h in range(2):
-            total = pa[y, hrows(h)]
-            for d in range(2):
-                n = ring_steps(ny, d, h)
-                if n > 0:
-                    rs_got(d, h, n)
-                    total = total + rb[d, h, n - 1].astype(F32)
-            for k in range(hw):
-                fin[h * hw + k] = total[k * R : (k + 1) * R]
-        row_exchange(lambda q: fin.at[q], ga_out.at[:, col(j)], S_GA)
 
         got(S_LRR)
         of = slw[0:1, :]
@@ -409,6 +399,17 @@
         )
         row_exchange(lambda q: vcs.at[q], vc.at[j], S_VC)
 
+        for h in range(2):
+            total = pa[y, hrows(h)]
+            for d in range(2):
+                n = ring_steps(ny, d, h)
+                if n > 0:
+                    rs_got(d, h, n)
+                    total = total + rb[d, h, n - 1].astype(F32)
+            for k in range(hw):
+                fin[h * hw + k] = total[k * R : (k + 1) * R].astype(BF)
+        row_exchange(lambda q: fin.at[q], gar.at[j], S_GA)
+
         got(S_TG)
         for k in range(rw):
             cols = slice(k * C, (k + 1) * C)
@@ -419,6 +420,8 @@
         got(S_GB)
         gb_out[...] = sum_of(gbp, ny)
         got(S_GA)
+        for k in range(rw):
+            ga_out[:, k * C : (k + 1) * C] = gar[k].astype(F32)
 
     work()
 
@@ -434,6 +437,15 @@
             pltpu.make_async_copy(ref, ref, ss.at[one]).wait()
 
 
+def hand_over(*refs):
+    sems = refs[8]
+    copies = [pltpu.make_async_copy(refs[i], refs[4 + i], sems.at[i]) for i in range(4)]
+    for copy in copies:
+        copy.start()
+    for copy in copies:
+        copy.wait()
+
+
 def shards(nx, ny, nz, tokens, weight, down, up, dy, adapter, lengths, table):
     rw = 2 * nx
     f = rw * C
@@ -443,14 +455,15 @@
     anywhere = pl.BlockSpec(memory_space=pl.ANY)
     vmem = pl.BlockSpec(memory_space=pltpu.VMEM)
     smem = pl.BlockSpec(memory_space=pltpu.SMEM)
-    values, token_grad, grad_a, grad_b = pl.pallas_call(
+    outs = (
+        jax.ShapeDtypeStruct((T, C), BF),
+        jax.ShapeDtypeStruct((T, f), BF),
+        jax.ShapeDtypeStruct((R, f), F32),
+        jax.ShapeDtypeStruct((R, C), F32),
+    )
+    made = pl.pallas_call(
         functools.partial(kernel, nx, ny, nz),
-        out_shape=(
-            jax.ShapeDtypeStruct((T, C), BF),
-            jax.ShapeDtypeStruct((T, f), BF),
-            jax.ShapeDtypeStruct((R, f), F32),
-            jax.ShapeDtypeStruct((R, C), F32),
-        ),
+        out_shape=outs,
         in_specs=[anywhere] * 5 + [smem] * 3,
         out_specs=(vmem, vmem, vmem, vmem),
         scratch_shapes=[
@@ -493,7 +506,8 @@
             vm((ny, rw * R, C), F32),
             vm((ny, rw * R, C), BF),
             vm((2, 2, steps, hr, C), BF),
-            vm((rw, R, C), F32),
+            vm((rw, R, C), BF),
+            vm((rw, R, C), BF),
             pltpu.SemaphoreType.DMA((N_STAGES,)),
             pltpu.SemaphoreType.DMA((N_STAGES,)),
             pltpu.SemaphoreType.DMA((2, 2, steps)),
@@ -515,6 +529,13 @@
         lengths.reshape(-1),
         table,
     )
+    values, token_grad, grad_a, grad_b = pl.pallas_call(
+        hand_over,
+        out_shape=outs,
+        in_specs=[anywhere] * 4,
+        out_specs=(anywhere,) * 4,
+        scratch_shapes=[pltpu.SemaphoreType.DMA((4,))],
+    )(*made)
     return values, token_grad, jnp.swapaxes(grad_a, 0, 1)[None], grad_b[None]
 
 

time: 81.6 us -> 89.7 us (1.099)
  Pallas kernels: 74.6 us -> 88.9 us
  local copies, waits for them, and re-layouts: 6.09 us -> 0 us
    pallas_call x1 -> x2, Pallas kernels: 74.6 us -> 88.9 us  [the longest x1 69.9 us: shards(): pl.pallas_call(functools.partial(kernel, nx, ny, nz), out_shape=outs, in_...]
    unnamed x4 -> x0, local copies, waits for them, and re-layouts: 6.09 us -> none
where the time goes in v3:
time: 89.7 us; the launch traced here: 89.6 us
  Pallas kernels  88.9 us (99%)
    pallas_call x1, Pallas kernels, shards(): pl.pallas_call(functools.partial(kernel, nx, ny, nz), out_shape=outs, in_...  69.9 us
    pallas_call x1, Pallas kernels, shards(): pl.pallas_call(hand_over, out_shape=outs, in_specs=[anywhere] * 4, out_sp...  19 us

profile of v3, /device:TPU:1, one launch (start us, length us, event | category | flops | bytes accessed | tf_op | source)
XLA Modules:
  0.0 89.6 jit_solution(17199167893127488616)
XLA Ops:
  0.6 69.9 %shard_map.111 = (bf16[128,128]{1,0:T(8,128)(2,1)}, bf16[128,1024]{1,0:T(8,128)(2,1)}, f32[64,1024]{1,0:T(8,128)}, f32[64,128]{1,0:T(8,128)}) custom-call(bf16[128,1024]{1,0:T(8,128)(2,1)} %x_hbm.1, bf16[1024,1024]{1,0:T(8,128)(2,1)} %w_hbm.1, bf16[64,1024]{1,0:T(8,128)(2,1)} %bitcast.10, bf16[64,128]{1,0:T(8,128)(2,1)} %bitcast.11, ...), custom_call_target="tpu_custom_call" | custom-call | tf_op jit(solution)/shard_map/pallas_call | solution.py:464
  70.6 19.0 %shard_map.112 = (bf16[128,128]{1,0:T(8,128)(2,1)}, bf16[128,1024]{1,0:T(8,128)(2,1)}, f32[64,1024]{1,0:T(8,128)}, f32[64,128]{1,0:T(8,128)}) custom-call(bf16[128,128]{1,0:T(8,128)(2,1)} %get-tuple-element.12.refs_0_, bf16[128,1024]{1,0:T(8,128)(2,1)} %get-tuple-element.13.refs_1_, f32[64,1024]{1,0:T(8,128)} %get-tuple-element.14.refs_2_, ...), custom_call_target="tpu_custom_call" | custom-call | tf_op jit(solution)/shard_map/pallas_call | solution.py:532

commit v4 on v3

--- a/solution.py
+++ b/solution.py
@@ -461,9 +461,10 @@
         jax.ShapeDtypeStruct((R, f), F32),
         jax.ShapeDtypeStruct((R, C), F32),
     )
+    kept = tuple(pltpu.VMEM(o.shape, o.dtype) for o in outs)
     made = pl.pallas_call(
         functools.partial(kernel, nx, ny, nz),
-        out_shape=outs,
+        out_shape=kept,
         in_specs=[anywhere] * 5 + [smem] * 3,
         out_specs=(vmem, vmem, vmem, vmem),
         scratch_shapes=[
@@ -535,7 +536,7 @@
         in_specs=[anywhere] * 4,
         out_specs=(anywhere,) * 4,
         scratch_shapes=[pltpu.SemaphoreType.DMA((4,))],
-    )(*made)
+    )(*[pltpu.with_memory_space_constraint(one, pltpu.VMEM) for one in made])
     return values, token_grad, jnp.swapaxes(grad_a, 0, 1)[None], grad_b[None]
 
 

time: 89.7 us -> 70.7 us (0.79)
  Pallas kernels: 88.9 us -> 70 us
    pallas_call x1, Pallas kernels: 19 us -> 0.84 us  [shards(): pl.pallas_call(hand_over, out_shape=outs, in_specs=[anywhere] * 4, out_sp...]
where the time goes in v4:
time: 70.7 us; the launch traced here: 70.6 us
  Pallas kernels  70 us (99%)
    pallas_call x1, Pallas kernels, shards(): pl.pallas_call(functools.partial(kernel, nx, ny, nz), out_shape=kept, in_...  69.1 us

profile of v4, /device:TPU:1, one launch (start us, length us, event | category | flops | bytes accessed | tf_op | source)
XLA Modules:
  0.0 70.6 jit_solution(13549199024931703685)
XLA Ops:
  0.6 69.1 %shard_map.111 = (bf16[128,128]{1,0:T(8,128)(2,1)S(1)}, bf16[128,1024]{1,0:T(8,128)(2,1)S(1)}, f32[64,1024]{1,0:T(8,128)S(1)}, f32[64,128]{1,0:T(8,128)S(1)}) custom-call(bf16[128,1024]{1,0:T(8,128)(2,1)} %x_hbm.1, bf16[1024,1024]{1,0:T(8,128)(2,1)} %w_hbm.1, bf16[64,1024]{1,0:T(8,128)(2,1)} %bitcast.10, bf16[64,128]{1,0:T(8,128)(2,1)} %bitcast.11, ...), custom_call_target="tpu_custom_call" | custom-call | tf_op jit(solution)/shard_map/pallas_call | solution.py:465
  69.8 0.8 %shard_map.112 = (bf16[128,128]{1,0:T(8,128)(2,1)}, bf16[128,1024]{1,0:T(8,128)(2,1)}, f32[64,1024]{1,0:T(8,128)}, f32[64,128]{1,0:T(8,128)}) custom-call(bf16[128,128]{1,0:T(8,128)(2,1)S(1)} %get-tuple-element.12.refs_0_, bf16[128,1024]{1,0:T(8,128)(2,1)S(1)} %get-tuple-element.13.refs_1_, f32[64,1024]{1,0:T(8,128)S(1)} %get-tuple-element.14.refs_2_, ...), custom_call_target="tpu_custom_call" | custom-call | tf_op jit(solution)/shard_map/pallas_call | solution.py:533

commit v5 on v4

--- a/solution.py
+++ b/solution.py
@@ -88,23 +88,28 @@
             src_ref=src, dst_ref=dst, send_sem=s, recv_sem=r, device_id=dev, device_id_type=MESH
         )
 
-    def exchange(n, mine, dev, src, dst, stage):
-        @pl.loop(1, n)
-        def _(i):
-            q = lax.rem(mine + i, n)
-            rcopy(src(q), dst, ss.at[stage], rs.at[stage], dev(q)).start()
-
+    def partners(n, mine, dev):
+        order = sorted(range(1, n), key=lambda i: (-min(i, n - i), i))
+        return [(q, dev(q)) for q in [lax.rem(mine + i, n) for i in order]]
+
+    row_peers = partners(rw, j, lambda q: (row_dev(q), z))
+    y_peers = partners(ny, y, lambda q: (y_dev(q), z))
+    z_peers = partners(nz, z, lambda q: (me, q))
+
+    def exchange(peers, mine, src, dst, stage):
+        for q, dev in peers:
+            rcopy(src(q), dst, ss.at[stage], rs.at[stage], dev).start()
         pltpu.make_async_copy(src(mine), dst, rs.at[stage]).start()
         started.append(stage)
 
     def row_exchange(src, dst, stage):
-        exchange(rw, j, lambda q: (row_dev(q), z), src, dst, stage)
+        exchange(row_peers, j, src, dst, stage)
 
     def y_exchange(src, dst, stage):
-        exchange(ny, y, lambda q: (y_dev(q), z), src, dst, stage)
+        exchange(y_peers, y, src, dst, stage)
 
     def z_exchange(src, dst, stage):
-        exchange(nz, z, lambda q: (me, q), src, dst, stage)
+        exchange(z_peers, z, src, dst, stage)
 
     def got(stage):
         ref = arrives[stage][0]

time: 70.7 us -> 69.6 us (0.984)
  Pallas kernels: 70 us -> 68.8 us
    pallas_call x1, Pallas kernels: 69.1 us -> 68 us  [shards(): pl.pallas_call(functools.partial(kernel, nx, ny, nz), out_shape=kept, in_...]
where the time goes in v5:
time: 69.6 us; the launch traced here: 69.5 us
  Pallas kernels  68.8 us (99%)
    pallas_call x1, Pallas kernels, shards(): pl.pallas_call(functools.partial(kernel, nx, ny, nz), out_shape=kept, in_...  68 us

profile of v5, /device:TPU:1, one launch (start us, length us, event | category | flops | bytes accessed | tf_op | source)
XLA Modules:
  0.0 69.5 jit_solution(5291924287023395833)
XLA Ops:
  0.6 68.0 %shard_map.111 = (bf16[128,128]{1,0:T(8,128)(2,1)S(1)}, bf16[128,1024]{1,0:T(8,128)(2,1)S(1)}, f32[64,1024]{1,0:T(8,128)S(1)}, f32[64,128]{1,0:T(8,128)S(1)}) custom-call(bf16[128,1024]{1,0:T(8,128)(2,1)} %x_hbm.1, bf16[1024,1024]{1,0:T(8,128)(2,1)} %w_hbm.1, bf16[64,1024]{1,0:T(8,128)(2,1)} %bitcast.10, bf16[64,128]{1,0:T(8,128)(2,1)} %bitcast.11, ...), custom_call_target="tpu_custom_call" | custom-call | tf_op jit(solution)/shard_map/pallas_call | solution.py:470
  68.6 0.8 %shard_map.112 = (bf16[128,128]{1,0:T(8,128)(2,1)}, bf16[128,1024]{1,0:T(8,128)(2,1)}, f32[64,1024]{1,0:T(8,128)}, f32[64,128]{1,0:T(8,128)}) custom-call(bf16[128,128]{1,0:T(8,128)(2,1)S(1)} %get-tuple-element.12.refs_0_, bf16[128,1024]{1,0:T(8,128)(2,1)S(1)} %get-tuple-element.13.refs_1_, f32[64,1024]{1,0:T(8,128)S(1)} %get-tuple-element.14.refs_2_, ...), custom_call_target="tpu_custom_call" | custom-call | tf_op jit(solution)/shard_map/pallas_call | solution.py:538
